TPU v7x, 32 devices: a whole 2x2x4 slice. The times are simulated.
32 devices in a mesh: dp: 8 (over y, x, core), tensor: 4 (over z).
Axes of the slice: x: 2, y: 2, z: 4, core: 2. Of those that a mesh axis runs over, the one named last changes fastest.
Arguments:
- tokens: bfloat16 [16384, 1024], P(('dp', 'tensor')), may hold values from -6 to 6
- w_qkv: bfloat16 [1024, 3, 1024], P('dp', None, 'tensor'), may hold values from -0.25 to 0.25
- w_out: bfloat16 [1024, 1024], P('tensor', 'dp'), may hold values from -0.5 to 0.5
- w_in: bfloat16 [1024, 2, 2624], P('dp', None, 'tensor'), may hold values from -0.1875 to 0.1875
- w_down: bfloat16 [2624, 1024], P('tensor', 'dp'), may hold values from -0.125 to 0.125
- gain_attn: bfloat16 [1024], P('dp'), may hold values from 0.5 to 1.5
- gain_mlp: bfloat16 [1024], P('dp'), may hold values from 0.5 to 1.5
- grad_output: bfloat16 [16384, 1024], P(('dp', 'tensor')), may hold values from -6 to 6
Outputs:
- output: bfloat16 [16384, 1024], P(('dp', 'tensor'))
- grad_tokens: bfloat16 [16384, 1024], P(('dp', 'tensor'))
- grad_qkv: float32 [1024, 3, 1024], P('dp', None, 'tensor')
- grad_out: float32 [1024, 1024], P('tensor', 'dp')
- grad_in: float32 [1024, 2, 2624], P('dp', None, 'tensor')
- grad_down: float32 [2624, 1024], P('tensor', 'dp')
- grad_gain_attn: float32 [1024], P('dp')
- grad_gain_mlp: float32 [1024], P('dp')
All inputs are finite; a program needn't handle non-finite values.
Results may differ from a plain program's by a relative error of at most 0.017.
The roundings to bfloat16 on the way count: a program that leaves them out, or rounds other values in their place, can miss the bound.
Values may be sent and summed in bfloat16 or wider, within the bound.
A program may use at most 192 MiB of HBM per device.

v0:
```python
import jax
import jax.numpy as jnp
from jax import lax
from jax.sharding import PartitionSpec as P

HD = 64
LEN = 1024
EPS = 1e-05
THETA = 160000.0


def layer_norm(values, gain):
    centred = values - jnp.mean(values, axis=-1, keepdims=True)
    spread = jnp.mean(centred * centred, axis=-1, keepdims=True)
    return centred * lax.rsqrt(spread + EPS) * gain


def rotary(values, length):
    rows = values.shape[0]
    half = values.shape[-1] // 2
    freq = THETA ** (-(jnp.arange(half).astype(jnp.float32) * 2.0 / values.shape[-1]))
    place = (jnp.arange(rows) % length).astype(jnp.float32)
    angle = place[:, None] * freq[None, :]
    cosine = jnp.cos(angle)[:, None, :]
    sine = jnp.sin(angle)[:, None, :]
    first = values[..., :half]
    second = values[..., half:]
    return jnp.concatenate(
        [first * cosine - second * sine, second * cosine + first * sine], axis=-1
    )


def geglu(pair):
    return jax.nn.gelu(pair[:, 0], approximate=False) * pair[:, 1]


def rotate_seq(values):
    return rotary(values, LEN)


def attend(query, key, value, length):
    rows, heads, size = query.shape
    block = min(512, length)
    scale = size ** (-0.5)

    def single(index):
        start = index * block
        first = start // length * length
        query_block = lax.dynamic_slice_in_dim(query, start, block, 0)
        key_seq = lax.dynamic_slice_in_dim(key, first, length, 0)
        value_seq = lax.dynamic_slice_in_dim(value, first, length, 0)
        scores = (
            jnp.einsum("qhe,khe->hqk", query_block, key_seq, preferred_element_type=jnp.float32)
            * scale
        )
        highest = jnp.max(scores, axis=-1, keepdims=True)
        total = jnp.sum(jnp.exp(scores - highest), axis=-1, keepdims=True)
        lse = highest + jnp.log(total)
        probs = jnp.exp(scores - lse).astype(jnp.bfloat16)
        result = jnp.einsum("hqk,khe->qhe", probs, value_seq, preferred_element_type=jnp.float32)
        return (result, lse[..., 0])

    results, lses = lax.map(single, jnp.arange(rows // block))
    return (results.reshape(rows, heads, size), lses)


def attend_back(query, key, value, lses, grad_att, length):
    rows, heads, size = query.shape
    block = min(512, length)
    scale = size ** (-0.5)
    zeros = jnp.zeros((rows, heads, size), jnp.float32)

    def step(index, carry):
        grad_query, grad_key, grad_value = carry
        start = index * block
        first = start // length * length
        query_block = lax.dynamic_slice_in_dim(query, start, block, 0)
        grad_block = lax.dynamic_slice_in_dim(grad_att, start, block, 0)
        key_seq = lax.dynamic_slice_in_dim(key, first, length, 0)
        value_seq = lax.dynamic_slice_in_dim(value, first, length, 0)
        lse = lax.dynamic_index_in_dim(lses, index, 0, keepdims=False)
        scores = (
            jnp.einsum("qhe,khe->hqk", query_block, key_seq, preferred_element_type=jnp.float32)
            * scale
        )
        probs = jnp.exp(scores - lse[..., None])
        dprob = jnp.einsum(
            "qhe,khe->hqk", grad_block, value_seq, preferred_element_type=jnp.float32
        )
        inner = jnp.sum(dprob * probs, axis=-1, keepdims=True)
        grad_scores = (probs * (dprob - inner)).astype(jnp.bfloat16)
        part_query = (
            jnp.einsum("hqk,khe->qhe", grad_scores, key_seq, preferred_element_type=jnp.float32)
            * scale
        )
        part_key = (
            jnp.einsum("hqk,qhe->khe", grad_scores, query_block, preferred_element_type=jnp.float32)
            * scale
        )
        part_value = jnp.einsum(
            "hqk,qhe->khe",
            probs.astype(jnp.bfloat16),
            grad_block,
            preferred_element_type=jnp.float32,
        )
        grad_query = lax.dynamic_update_slice_in_dim(grad_query, part_query, start, 0)
        grad_key = lax.dynamic_update_slice_in_dim(
            grad_key, lax.dynamic_slice_in_dim(grad_key, first, length, 0) + part_key, first, 0
        )
        grad_value = lax.dynamic_update_slice_in_dim(
            grad_value,
            lax.dynamic_slice_in_dim(grad_value, first, length, 0) + part_value,
            first,
            0,
        )
        return (grad_query, grad_key, grad_value)

    return lax.fori_loop(0, rows // block, step, (zeros, zeros, zeros))


def local(tokens, w_qkv, w_out, w_in, w_down, gain_attn, gain_mlp, grad_output):
    gathered_w = (
        lax.all_gather(w_qkv, "dp", axis=0, tiled=True),
        lax.all_gather(w_out, "dp", axis=1, tiled=True),
        lax.all_gather(w_in, "dp", axis=0, tiled=True),
        lax.all_gather(w_down, "dp", axis=1, tiled=True),
        lax.all_gather(gain_attn, "dp", axis=0, tiled=True),
        lax.all_gather(gain_mlp, "dp", axis=0, tiled=True),
    )
    qkv_w, out_w, in_w, down_w, gain_first, gain_second = gathered_w
    gain_one = gain_first.astype(jnp.float32)
    gain_two = gain_second.astype(jnp.float32)
    inputs = tokens.astype(jnp.float32)
    normed_one = layer_norm(inputs, gain_one).astype(jnp.bfloat16)
    gathered_one = lax.all_gather(normed_one, "tensor", axis=0, tiled=True)
    rows = gathered_one.shape[0]
    heads = qkv_w.shape[2] // HD
    projected = jnp.einsum("td,dcf->tcf", gathered_one, qkv_w, preferred_element_type=jnp.float32)
    split = projected.reshape(rows, 3, heads, HD)
    query_f = split[:, 0]
    query_b = rotary(query_f, LEN).astype(jnp.bfloat16)
    key_b = rotary(split[:, 1], LEN).astype(jnp.bfloat16)
    value_b = split[:, 2].astype(jnp.bfloat16)
    attended, lses = attend(query_b, key_b, value_b, LEN)
    attended_b = attended.reshape(rows, heads * HD).astype(jnp.bfloat16)
    branch_one = lax.psum_scatter(
        jnp.dot(attended_b, out_w, preferred_element_type=jnp.float32),
        "tensor",
        scatter_dimension=0,
        tiled=True,
    )
    residual = inputs + branch_one
    normed_two = layer_norm(residual, gain_two).astype(jnp.bfloat16)
    gathered_two = lax.all_gather(normed_two, "tensor", axis=0, tiled=True)
    pair = jnp.einsum("td,dcf->tcf", gathered_two, in_w, preferred_element_type=jnp.float32)
    hidden = geglu(pair).astype(jnp.bfloat16)
    branch_two = lax.psum_scatter(
        jnp.dot(hidden, down_w, preferred_element_type=jnp.float32).astype(jnp.bfloat16),
        "tensor",
        scatter_dimension=0,
        tiled=True,
    ).astype(jnp.float32)
    output = (residual + branch_two).astype(jnp.bfloat16)
    regathered = (
        lax.all_gather(w_qkv, "dp", axis=0, tiled=True),
        lax.all_gather(w_out, "dp", axis=1, tiled=True),
        lax.all_gather(w_in, "dp", axis=0, tiled=True),
        lax.all_gather(w_down, "dp", axis=1, tiled=True),
        lax.all_gather(gain_attn, "dp", axis=0, tiled=True),
        lax.all_gather(gain_mlp, "dp", axis=0, tiled=True),
    )
    qkv_w, out_w, in_w, down_w, gain_first, gain_second = regathered
    gain_one = gain_first.astype(jnp.float32)
    gain_two = gain_second.astype(jnp.float32)
    grad_top = grad_output.astype(jnp.float32)
    grad_all = lax.all_gather(grad_output, "tensor", axis=0, tiled=True)
    grad_down = jnp.einsum("tf,td->fd", hidden, grad_all, preferred_element_type=jnp.float32)
    grad_hidden = jnp.einsum("td,fd->tf", grad_all, down_w, preferred_element_type=jnp.float32)
    geglu_pull = jax.vjp(geglu, pair)[1]
    grad_pair = geglu_pull(grad_hidden)[0].astype(jnp.bfloat16)
    grad_in = jnp.einsum("td,tcf->dcf", gathered_two, grad_pair, preferred_element_type=jnp.float32)
    grad_normed_two = lax.psum_scatter(
        jnp.einsum("tcf,dcf->td", grad_pair, in_w, preferred_element_type=jnp.float32),
        "tensor",
        scatter_dimension=0,
        tiled=True,
    )
    norm_pull_two = jax.vjp(layer_norm, residual, gain_two)[1]
    grad_res_part, grad_gain_two = norm_pull_two(grad_normed_two)
    grad_residual = grad_top + grad_res_part
    grad_res_b = grad_residual.astype(jnp.bfloat16)
    grad_res_all = lax.all_gather(grad_res_b, "tensor", axis=0, tiled=True)
    grad_out_w = jnp.einsum(
        "tf,td->fd", attended_b, grad_res_all, preferred_element_type=jnp.float32
    )
    grad_att = jnp.einsum("td,fd->tf", grad_res_all, out_w, preferred_element_type=jnp.float32)
    grad_att = grad_att.astype(jnp.bfloat16).reshape(rows, heads, HD)
    grad_query, grad_key, grad_value = attend_back(query_b, key_b, value_b, lses, grad_att, LEN)
    rotary_pull = jax.vjp(rotate_seq, query_f)[1]
    back_query = rotary_pull(grad_query)[0]
    back_key = rotary_pull(grad_key)[0]
    grad_proj = (
        jnp.stack([back_query, back_key, grad_value], axis=1)
        .reshape(rows, 3, heads * HD)
        .astype(jnp.bfloat16)
    )
    grad_qkv_w = jnp.einsum(
        "td,tcf->dcf", gathered_one, grad_proj, preferred_element_type=jnp.float32
    )
    grad_normed_one = lax.psum_scatter(
        jnp.einsum("tcf,dcf->td", grad_proj, qkv_w, preferred_element_type=jnp.float32),
        "tensor",
        scatter_dimension=0,
        tiled=True,
    )
    norm_pull_one = jax.vjp(layer_norm, inputs, gain_one)[1]
    grad_in_part, grad_gain_one = norm_pull_one(grad_normed_one)
    grad_tokens = (grad_residual + grad_in_part).astype(jnp.bfloat16)
    summed = (
        lax.psum_scatter(grad_qkv_w, "dp", scatter_dimension=0, tiled=True),
        lax.psum_scatter(grad_out_w, "dp", scatter_dimension=1, tiled=True),
        lax.psum_scatter(grad_in, "dp", scatter_dimension=0, tiled=True),
        lax.psum_scatter(grad_down, "dp", scatter_dimension=1, tiled=True),
        lax.psum_scatter(grad_gain_one, "dp", scatter_dimension=0, tiled=True),
        lax.psum_scatter(grad_gain_two, "dp", scatter_dimension=0, tiled=True),
    )
    gain_first_grad, gain_second_grad = lax.psum((summed[4], summed[5]), "tensor")
    return (
        output,
        grad_tokens,
        summed[0],
        summed[1],
        summed[2],
        summed[3],
        gain_first_grad,
        gain_second_grad,
    )


def solution(mesh):
    placed = (
        P(("dp", "tensor"), None),
        P("dp", None, "tensor"),
        P("tensor", "dp"),
        P("dp", None, "tensor"),
        P("tensor", "dp"),
        P("dp"),
        P("dp"),
        P(("dp", "tensor"), None),
    )
    return jax.shard_map(
        local,
        mesh=mesh,
        in_specs=placed,
        out_specs=(
            P(("dp", "tensor"), None),
            P(("dp", "tensor"), None),
            P("dp", None, "tensor"),
            P("tensor", "dp"),
            P("dp", None, "tensor"),
            P("tensor", "dp"),
            P("dp"),
            P("dp"),
        ),
        check_vma=False,
    )
```

profile of v0, /device:TPU:0, one launch (start us, length us, event | category | flops | bytes accessed | tf_op | source)
XLA Modules:
  0.0 1317.4 jit_solution(13067545842820573546)
XLA Ops:
  9.0 10.3 all-gather
  23.7 2.6 fusion.78
  26.4 12.3 all_gather.39
  40.5 82.9 %all-gather.10.cloned.1.call-done = bf16[2048,1024]{1,0:T(8,128)(2,1)} async-done(((bf16[512,1024]{1,0:T(8,128)(2,1)}), bf16[2048,1024]{1,0:T(8,128)(2,1)}) %all-gather.10.cloned.1.call-update) | async-done | bytes 4194320 | tf_op jit(solution)/shard_map/all_gather | solution.py:135
  123.4 5.7 fusion.70
  130.6 29.7 %while.33 = (s32[]{:T(128)}, bf16[4,512,4,64]{1,3,2,0:T(8,128)(2,1)}, f32[4,4,512]{2,1,0:T(4,128)S(1)}, s32[4]{0:T(128)S(1)}, bf16[2048,4,64]{0,2,1:T(8,128)(2,1...) while((s32[]{:T(128)}, ...), condition=%wide.region_5.6_spmd, body=%wide.region_2.5_spmd.sunk | while | flops 553646080 | bytes 35455444 | solution.py:63
  160.4 2.8 copy.30
  164.4 4.6 fusion.98
  170.8 9.0 all-gather.1
  179.8 132.3 %reduce-scatter.9.cloned.1.call-done = f32[512,1024]{1,0:T(8,128)} async-done(((f32[2048,1024]{1,0:T(8,128)}), f32[512,1024]{1,0:T(8,128)}) %reduce-scatter.9.cloned.1.call-update) | async-done | bytes 2097168 | tf_op jit(solution)/shard_map/reduce_scatter | solution.py:146
  312.2 2.1 fusion.97
  316.0 23.5 %all-gather.18.cloned.1.call-done = bf16[656,1024]{1,0:T(8,128)(2,1)} async-done(((bf16[656,128]{1,0:T(8,128)(2,1)}), bf16[656,1024]{1,0:T(8,128)(2,1)}) %all-gather.18.cloned.1.call-update) | async-done | bytes 1343504 | tf_op jit(solution)/shard_map/all_gather | solution.py:126
  339.5 82.2 %all-gather.20.cloned.1.call-done = bf16[2048,1024]{1,0:T(8,128)(2,1)} async-done(((bf16[512,1024]{1,0:T(8,128)(2,1)}), bf16[2048,1024]{1,0:T(8,128)(2,1)}) %all-gather.20.cloned.1.call-update) | async-done | bytes 4194320 | tf_op jit(solution)/shard_map/all_gather | solution.py:176
  421.7 7.9 fusion.99
  429.7 23.2 %all-gather.16.cloned.1.call-done = bf16[1024,2,656]{0,2,1:T(8,128)(2,1)} async-done(((bf16[128,2,656]{0,2,1:T(8,128)(2,1)}), bf16[1024,2,656]{0,2,1:T(8,128)(2,1)}) %all-gather.16.cloned.1.call-update) | async-done | bytes 2686992 | tf_op jit(solution)/shard_map/all_gather | solution.py:125
  452.8 82.9 %all-gather.14.cloned.1.call-done = bf16[2048,1024]{1,0:T(8,128)(2,1)} async-done(((bf16[512,1024]{1,0:T(8,128)(2,1)}), bf16[2048,1024]{1,0:T(8,128)(2,1)}) %all-gather.14.cloned.1.call-update) | async-done | bytes 4194320 | tf_op jit(solution)/shard_map/all_gather | solution.py:154
  535.8 8.5 fusion.66
  544.3 12.5 multiply_bitcast_fusion
  556.8 5.2 fusion.51
  562.0 13.5 %convolution_bitcast_fusion.1 = f32[2048,1024]{1,0:T(8,128)} fusion(bf16[1024,2,656]{0,2,1:T(8,128)(2,1)} %all-gather.16.cloned.1.call-done, f32[2048,1,656]{0,2,1:T(8,128)} %get-tuple-element.379, f32[2048,1,656]{0,2,1:T(8,128)} %get-tuple-element.371), kind=kOutput, calls=%fused_computation.82 | convolution fusion | flops 5508300800 | bytes 21823488 | tf_op jit(solution)/shard_map/tcf,dcf->td/dot_general | solution.py:183
  575.6 11.9 reduce-scatter.11.cloned.1.call-start
  587.5 7.7 convolution_convert_fusion
  595.2 123.5 %reduce-scatter.13.cloned.1.call-done = f32[512,1024]{1,0:T(8,128)} async-done(((f32[2048,1024]{1,0:T(8,128)}), f32[512,1024]{1,0:T(8,128)}) %reduce-scatter.13.cloned.1.call-update) | async-done | bytes 2097168 | tf_op jit(solution)/shard_map/reduce_scatter | solution.py:182
  718.7 2.8 multiply_reduce_fusion.2
  721.6 77.0 %reduce-scatter.11.cloned.1.call-done = bf16[512,1024]{1,0:T(8,128)(2,1)} async-done(((bf16[2048,1024]{1,0:T(8,128)(2,1)}), bf16[512,1024]{1,0:T(8,128)(2,1)}) %reduce-scatter.11.cloned.1.call-update) | async-done | bytes 1048592 | tf_op jit(solution)/shard_map/reduce_scatter | solution.py:157
  798.5 3.7 fusion.95
  805.0 81.4 %all-gather.22.cloned.1.call-done = bf16[2048,1024]{1,0:T(8,128)(2,1)} async-done(((bf16[512,1024]{1,0:T(8,128)(2,1)}), bf16[2048,1024]{1,0:T(8,128)(2,1)}) %all-gather.22.cloned.1.call-update) | async-done | bytes 4194320 | tf_op jit(solution)/shard_map/all_gather | solution.py:192
  886.4 4.4 convolution_convert_fusion.1
  894.2 53.7 %while.34 = (s32[]{:T(128)}, f32[2048,4,64]{0,2,1:T(8,128)}, f32[2048,4,64]{0,2,1:T(8,128)S(1)}, f32[2048,4,64]{0,2,1:T(8,128)}, bf16[2048,4,64]{0,2,1:T(8,128)(...) while((s32[]{:T(128)}, f32[2048,4,64]{0,2,1:T(8,128)}, ...), condition=%wide.region_15.16_spmd, body=%wide.region_13.15_spmd.sunk | while | flops 1368258560 | bytes 95478312 | solution.py:118
  894.2 2.4 fusion.144
  898.6 2.9 multiply_reduce_fusion.8
  901.4 2.0 multiply_convert_fusion.4
  903.5 1.9 fusion.146
  905.4 2.2 fusion.145
  907.7 2.4 fusion.144
  912.0 2.8 multiply_reduce_fusion.8
  914.9 2.0 multiply_convert_fusion.4
  916.9 1.9 fusion.146
  918.9 2.2 fusion.145
  921.1 2.4 fusion.144
  925.4 2.9 multiply_reduce_fusion.8
  928.3 2.0 multiply_convert_fusion.4
  930.3 1.9 fusion.146
  932.3 2.2 fusion.145
  934.5 2.4 fusion.144
  938.9 2.8 multiply_reduce_fusion.8
  941.7 2.0 multiply_convert_fusion.4
  943.8 1.9 fusion.146
  945.7 2.2 fusion.145
  951.0 3.3 multiply_add_fusion.3
  956.5 9.1 convolution_bitcast_fusion
  967.3 6.6 fusion.101
  974.0 11.2 fusion.64
  986.5 4.4 fusion.100
  991.0 7.7 fusion.68
  1000.1 108.7 %reduce-scatter.15.cloned.1.call-done = f32[512,1024]{1,0:T(8,128)} async-done(((f32[2048,1024]{1,0:T(8,128)}), f32[512,1024]{1,0:T(8,128)}) %reduce-scatter.15.cloned.1.call-update) | async-done | bytes 2097168 | tf_op jit(solution)/shard_map/reduce_scatter | solution.py:210
  1108.8 2.2 fusion.81
  1112.1 13.7 %all-reduce.8 = (f32[1024]{0:T(1024)S(1)}, f32[1024]{0:T(1024)S(1)}) all-reduce(f32[1024]{0:T(1024)S(1)} %get-tuple-element.329, f32[1024]{0:T(1024)S(1)} %copy-done.37), channel_id=10, replica_groups=mesh['dp'=8,'tensor'=4] {'dp'}, use_global_device_ids=true, to_apply=%region_24.25.clone | all-reduce | flops 2048 | bytes 16384
  1125.9 12.1 all-reduce.9
  1138.1 3.2 add_convert_fusion.1
  1141.3 17.2 %reduce-scatter.23.cloned.1.call-done = f32[656,128]{1,0:T(8,128)} async-done(((f32[656,1024]{1,0:T(8,128)}), f32[656,128]{1,0:T(8,128)}) %reduce-scatter.23.cloned.1.call-update) | async-done | bytes 335888 | tf_op jit(solution)/shard_map/reduce_scatter | solution.py:223
  1158.5 61.6 %reduce-scatter.21.cloned.1.call-done = f32[128,2,656]{0,2,1:T(8,128)} async-done(((f32[1024,2,656]{0,2,1:T(8,128)}), f32[128,2,656]{0,2,1:T(8,128)}) %reduce-scatter.21.cloned.1.call-update) | async-done | bytes 671760 | tf_op jit(solution)/shard_map/reduce_scatter | solution.py:222
  1220.1 40.0 %reduce-scatter.19.cloned.1.call-done = f32[256,128]{1,0:T(8,128)} async-done(((f32[256,1024]{1,0:T(8,128)}), f32[256,128]{1,0:T(8,128)}) %reduce-scatter.19.cloned.1.call-update) | async-done | bytes 131088 | tf_op jit(solution)/shard_map/reduce_scatter | solution.py:221
  1260.1 50.5 %reduce-scatter.17.cloned.1.call-done = f32[128,3,256]{2,0,1:T(8,128)} async-done(((f32[1024,3,256]{2,0,1:T(8,128)}), f32[128,3,256]{2,0,1:T(8,128)}) %reduce-scatter.17.cloned.1.call-update) | async-done | bytes 393232 | tf_op jit(solution)/shard_map/reduce_scatter | solution.py:220
  (214 shorter events, 65.0 us)
Async XLA Ops:
  7.2 19.2 %copy-start.30 = (bf16[256,128]{1,0:T(8,128)(2,1)S(1)}, bf16[256,128]{1,0:T(8,128)(2,1)}, u32[]{:S(2)}) copy-start(bf16[256,128]{1,0:T(8,128)(2,1)} %param.14) | copy-start | bytes 196612
  7.2 33.4 %all-gather.12.cloned.1.call-start = ((), (), s32[]{:S(2)}) async-start(), calls=%async_computation.9 | async-start | bytes 1769472 | tf_op jit(solution)/shard_map/all_gather | solution.py:123
  9.0 114.4 %all-gather.10.cloned.1.call-start = ((), (), s32[]{:S(2)}) async-start(), calls=%async_computation.8 | async-start | bytes 5242880 | tf_op jit(solution)/shard_map/all_gather | solution.py:135
  19.4 3.7 copy-start.26
  20.8 2.3 copy-start.28
  26.3 285.9 %reduce-scatter.9.cloned.1.call-start = ((), (), s32[]{:S(2)}) async-start(), calls=%async_computation.10 | async-start | bytes 10485760 | tf_op jit(solution)/shard_map/reduce_scatter | solution.py:146
  39.7 90.1 %copy-start.16 = (f32[2048,32]{0,1:T(8,128)}, f32[2048,32]{0,1:T(8,128)S(1)}, u32[]{:S(2)}) copy-start(f32[2048,32]{0,1:T(8,128)S(1)} %get-tuple-element.396) | copy-start | bytes 786436
  39.7 90.1 %copy-start.18 = (f32[2048,32]{0,1:T(8,128)}, f32[2048,32]{0,1:T(8,128)S(1)}, u32[]{:S(2)}) copy-start(f32[2048,32]{0,1:T(8,128)S(1)} %get-tuple-element.397) | copy-start | bytes 786436
  133.3 1.9 copy-start.24
  140.7 1.9 copy-start.24
  148.2 1.9 copy-start.24
  155.6 1.9 copy-start.24
  160.4 8.6 copy-start.3
  160.4 8.6 copy-start.5
  160.4 4.1 copy-start.19
  169.0 1.8 copy-start.38
  169.0 170.5 %all-gather.18.cloned.1.call-start = ((), (), s32[]{:S(2)}) async-start(), calls=%async_computation.13 | async-start | bytes 1511424 | tf_op jit(solution)/shard_map/all_gather | solution.py:126
  169.6 252.1 %all-gather.20.cloned.1.call-start = ((), (), s32[]{:S(2)}) async-start(), calls=%async_computation.15 | async-start | bytes 5242880 | tf_op jit(solution)/shard_map/all_gather | solution.py:176
  170.2 282.6 %all-gather.16.cloned.1.call-start = ((), (), s32[]{:S(2)}) async-start(), calls=%async_computation.12 | async-start | bytes 3022848 | tf_op jit(solution)/shard_map/all_gather | solution.py:125
  170.8 365.0 %all-gather.14.cloned.1.call-start = ((), (), s32[]{:S(2)}) async-start(), calls=%async_computation.11 | async-start | bytes 5242880 | tf_op jit(solution)/shard_map/all_gather | solution.py:154
  316.0 402.7 %reduce-scatter.13.cloned.1.call-start = ((), (), s32[]{:S(2)}) async-start(), calls=%async_computation.16 | async-start | bytes 10485760 | tf_op jit(solution)/shard_map/reduce_scatter | solution.py:182
  535.8 8.6 copy-start.6
  575.6 223.0 %reduce-scatter.11.cloned.1.call-start = ((), (), s32[]{:S(2)}) async-start(), calls=%async_computation.14 | async-start | bytes 5242880 | tf_op jit(solution)/shard_map/reduce_scatter | solution.py:157
  595.2 291.2 %all-gather.22.cloned.1.call-start = ((), (), s32[]{:S(2)}) async-start(), calls=%async_computation.17 | async-start | bytes 5242880 | tf_op jit(solution)/shard_map/all_gather | solution.py:192
  798.5 5.1 copy-start.10
  802.2 84.1 %copy-start.20 = (bf16[256,1024]{1,0:T(8,128)(2,1)S(1)}, bf16[256,1024]{1,0:T(8,128)(2,1)}, u32[]{:S(2)}) copy-start(bf16[256,1024]{1,0:T(8,128)(2,1)} %all_gather.39) | copy-start | bytes 1572868
  802.2 88.6 %copy-start.33 = (f32[512]{0:T(512)}, f32[512]{0:T(512)S(1)}, u32[]{:S(2)}) copy-start(f32[512]{0:T(512)S(1)} %negate_multiply_fusion.2) | copy-start | bytes 6148
  804.9 303.9 %reduce-scatter.15.cloned.1.call-start = ((), (), s32[]{:S(2)}) async-start(), calls=%async_computation.18 | async-start | bytes 10485760 | tf_op jit(solution)/shard_map/reduce_scatter | solution.py:210
  894.2 2.4 copy-start.1
  894.2 2.4 copy-start.11
  896.6 1.9 copy-start.4
  898.5 2.9 copy-start.2
  907.7 2.4 copy-start.1
  907.7 2.4 copy-start.11
  910.1 1.9 copy-start.4
  912.0 2.9 copy-start.2
  921.1 2.4 copy-start.1
  921.1 2.4 copy-start.11
  923.5 1.9 copy-start.4
  925.4 2.9 copy-start.2
  934.5 2.4 copy-start.1
  934.5 2.4 copy-start.11
  936.9 1.9 copy-start.4
  938.8 2.9 copy-start.2
  947.9 3.1 copy-start.17
  954.3 1.5 copy-start.14
  956.4 9.1 copy-start.23
  965.6 1.8 copy-start.15
  965.6 192.8 %reduce-scatter.23.cloned.1.call-start = ((), (), s32[]{:S(2)}) async-start(), calls=%async_computation.22 | async-start | bytes 3022848 | tf_op jit(solution)/shard_map/reduce_scatter | solution.py:223
  974.0 246.1 %reduce-scatter.21.cloned.1.call-start = ((), (), s32[]{:S(2)}) async-start(), calls=%async_computation.21 | async-start | bytes 6045696 | tf_op jit(solution)/shard_map/reduce_scatter | solution.py:222
  985.3 5.7 copy-start.21
  985.3 5.7 copy-start.22
  985.3 274.8 %reduce-scatter.19.cloned.1.call-start = ((), (), s32[]{:S(2)}) async-start(), calls=%async_computation.20 | async-start | bytes 1179648 | tf_op jit(solution)/shard_map/reduce_scatter | solution.py:221
  990.9 7.9 copy-start.39
  990.9 117.9 %copy-start = (bf16[512,1024]{1,0:T(8,128)(2,1)S(1)}, bf16[512,1024]{1,0:T(8,128)(2,1)}, u32[]{:S(2)}) copy-start(bf16[512,1024]{1,0:T(8,128)(2,1)} %param.12) | copy-start | bytes 3145732
  990.9 117.9 %copy-start.27 = (f32[8,1,128]{2,1,0:T(1,128)S(1)}, f32[8,1,128]{2,1,0:T(1,128)}, u32[]{:S(2)}) copy-start(f32[8,1,128]{2,1,0:T(1,128)} %copy-done.26) | copy-start | bytes 12292
  990.9 117.9 %copy-start.29 = (f32[512]{0:T(512)S(1)}, f32[512]{0:T(512)}, u32[]{:S(2)}) copy-start(f32[512]{0:T(512)} %copy-done.28) | copy-start | bytes 6148
  990.9 319.6 %reduce-scatter.17.cloned.1.call-start = ((), (), s32[]{:S(2)}) async-start(), calls=%async_computation.19 | async-start | bytes 3538944 | tf_op jit(solution)/shard_map/reduce_scatter | solution.py:220
  998.7 112.3 %copy-start.36 = (f32[512]{0:T(512)S(1)}, f32[512]{0:T(512)}, u32[]{:S(2)}) copy-start(f32[512]{0:T(512)} %copy-done.35) | copy-start | bytes 6148
  998.7 112.3 %copy-start.32 = (f32[512]{0:T(512)S(1)}, f32[512]{0:T(512)}, u32[]{:S(2)}) copy-start(f32[512]{0:T(512)} %copy-done.31) | copy-start | bytes 6148
  998.7 113.4 %copy-start.37 = (f32[1024]{0:T(1024)S(1)}, f32[1024]{0:T(1024)}, u32[]{:S(2)}) copy-start(f32[1024]{0:T(1024)} %get-tuple-element.327) | copy-start | bytes 12292
  998.7 139.3 %copy-start.8 = (f32[512,1024]{1,0:T(8,128)S(1)}, f32[512,1024]{1,0:T(8,128)}, u32[]{:S(2)}) copy-start(f32[512,1024]{1,0:T(8,128)} %copy-done.7) | copy-start | bytes 6291460
  998.7 139.3 %copy-start.34 = (f32[512]{0:T(512)S(1)}, f32[512]{0:T(512)}, u32[]{:S(2)}) copy-start(f32[512]{0:T(512)} %copy-done.33) | copy-start | bytes 6148
  1108.8 2.3 copy-start.9
  (9 other events, 8.6 us)
Sparse Core Ops, SparseCore 0:
  10.5 30.0 all-gather.11
  42.7 80.7 all-gather.9
  169.1 142.9 reduce-scatter.8
  313.9 25.5 all-gather.17
  340.9 80.7 all-gather.19
  423.5 29.3 all-gather.15
  455.0 80.7 all-gather.13
  575.7 142.9 reduce-scatter.12
  721.0 77.4 reduce-scatter.10
  805.0 81.2 all-gather.21
  965.7 142.9 reduce-scatter.14
  1113.0 45.3 reduce-scatter.22
  1162.8 57.1 reduce-scatter.20
  1224.0 36.0 reduce-scatter.18
  1264.3 46.2 reduce-scatter.16
where the time goes:
time: 1330 us; the launch traced here: 1320 us
  waiting for transfers between devices  989 us (74%)
  matrix products  150 us (11%)
  other arithmetic  64.2 us (5%)
  blocking collectives  57.4 us (4%)
  local copies, waits for them, and re-layouts  25.2 us (2%)
  between operations  15.4 us (1%)
    reduce_scatter x1, waiting for transfers between devices, local(): lax.psum_scatter(jnp.dot(attended_b, out_w, preferred_element_type=jnp.fl...  132 us
    reduce_scatter x1, waiting for transfers between devices, local(): lax.psum_scatter(jnp.einsum('tcf,dcf->td', grad_pair, in_w, preferred_ele...  124 us
    reduce_scatter x1, waiting for transfers between devices, local(): lax.psum_scatter(jnp.einsum('tcf,dcf->td', grad_proj, qkv_w, preferred_el...  109 us
    all_gather x1, waiting for transfers between devices, local(): gathered_two = lax.all_gather(normed_two, 'tensor', axis=0, tiled=True)  82.9 us
    all_gather x1, waiting for transfers between devices, local(): gathered_one = lax.all_gather(normed_one, 'tensor', axis=0, tiled=True)  82.9 us
    all_gather x1, waiting for transfers between devices, local(): grad_all = lax.all_gather(grad_output, 'tensor', axis=0, tiled=True)  82.2 us
    all_gather x1, waiting for transfers between devices, local(): grad_res_all = lax.all_gather(grad_res_b, 'tensor', axis=0, tiled=True)  81.4 us
    reduce_scatter x1, waiting for transfers between devices, local(): lax.psum_scatter(jnp.dot(hidden, down_w, preferred_element_type=jnp.float...  77 us
  transfers between devices with their start and end apart: 15, of which 15 were waited for; matrix products, arithmetic and copies ran while one was open for 5% of the time, Pallas kernels for 0%

commit v1 on v0

--- a/solution.py
+++ b/solution.py
@@ -173,7 +173,14 @@
     gain_one = gain_first.astype(jnp.float32)
     gain_two = gain_second.astype(jnp.float32)
     grad_top = grad_output.astype(jnp.float32)
-    grad_all = lax.all_gather(grad_output, "tensor", axis=0, tiled=True)
+    ring = [grad_output]
+    for hop in range(3):
+        ring.append(lax.ppermute(ring[-1], "tensor", [(dev, (dev + 1) % 4) for dev in range(4)]))
+    grad_all = jnp.roll(
+        jnp.concatenate(ring[::-1], axis=0),
+        (lax.axis_index("tensor") + 1) * ring[0].shape[0],
+        axis=0,
+    )
     grad_down = jnp.einsum("tf,td->fd", hidden, grad_all, preferred_element_type=jnp.float32)
     grad_hidden = jnp.einsum("td,fd->tf", grad_all, down_w, preferred_element_type=jnp.float32)
     geglu_pull = jax.vjp(geglu, pair)[1]

time: 1330 us -> 1260 us (0.947)
  waiting for transfers between devices: 989 us -> 900 us
    ppermute x0 -> x3, waiting for transfers between devices: none -> 87.3 us  [local(): lax.ppermute(ring[-1], 'tensor', [(dev, (dev + 1) % 4) for dev in range(4)])]
    all_gather x1 -> x0, waiting for transfers between devices: 82.2 us -> none  [local(): grad_all = lax.all_gather(grad_output, 'tensor', axis=0, tiled=True)]
    all_gather x1, waiting for transfers between devices: 82.9 us -> 34.4 us  [local(): gathered_two = lax.all_gather(normed_two, 'tensor', axis=0, tiled=True)]
    all_gather x1, waiting for transfers between devices: 23.5 us -> 0.01 us  [local(): lax.all_gather(w_down, 'dp', axis=1, tiled=True)]
    all_gather x1, waiting for transfers between devices: 23.2 us -> 0.01 us  [local(): lax.all_gather(w_in, 'dp', axis=0, tiled=True)]
  transfers between devices with their start and end apart: 15 -> 17, of which waited for: 15 -> 15; matrix products, arithmetic and copies ran while one was open for 5% -> 7% of each run, Pallas kernels for 0% -> 0%
where the time goes in v1:
time: 1260 us; the launch traced here: 1250 us
  waiting for transfers between devices  900 us (71%)
  matrix products  152 us (12%)
  other arithmetic  65.7 us (5%)
  blocking collectives  56.8 us (5%)
  local copies, waits for them, and re-layouts  38.3 us (3%)
  between operations  15.5 us (1%)
  starting transfers between devices  14.1 us (1%)
    reduce_scatter x1, waiting for transfers between devices, local(): lax.psum_scatter(jnp.dot(attended_b, out_w, preferred_element_type=jnp.fl...  133 us
    reduce_scatter x1, waiting for transfers between devices, local(): lax.psum_scatter(jnp.einsum('tcf,dcf->td', grad_pair, in_w, preferred_ele...  123 us
    reduce_scatter x1, waiting for transfers between devices, local(): lax.psum_scatter(jnp.einsum('tcf,dcf->td', grad_proj, qkv_w, preferred_el...  109 us
    ppermute x3, waiting for transfers between devices, local(): lax.ppermute(ring[-1], 'tensor', [(dev, (dev + 1) % 4) for dev in range(4)])  87.3 us
    all_gather x1, waiting for transfers between devices, local(): gathered_one = lax.all_gather(normed_one, 'tensor', axis=0, tiled=True)  83.2 us
    all_gather x1, waiting for transfers between devices, local(): grad_res_all = lax.all_gather(grad_res_b, 'tensor', axis=0, tiled=True)  81.4 us
    reduce_scatter x1, waiting for transfers between devices, local(): lax.psum_scatter(jnp.dot(hidden, down_w, preferred_element_type=jnp.float...  77 us
    reduce_scatter x1, waiting for transfers between devices, local(): lax.psum_scatter(grad_in, 'dp', scatter_dimension=0, tiled=True)  61.5 us
  transfers between devices with their start and end apart: 17, of which 15 were waited for; matrix products, arithmetic and copies ran while one was open for 7% of the time, Pallas kernels for 0%

profile of v1, /device:TPU:0, one launch (start us, length us, event | category | flops | bytes accessed | tf_op | source)
XLA Modules:
  0.0 1245.3 jit_solution(6675823136121205539)
XLA Ops:
  9.0 10.3 all-gather
  22.5 2.6 fusion.82
  25.3 11.9 all_gather.36
  39.9 83.2 %all-gather.9.cloned.1.call-done = bf16[2048,1024]{1,0:T(8,128)(2,1)} async-done(((bf16[512,1024]{1,0:T(8,128)(2,1)}), bf16[2048,1024]{1,0:T(8,128)(2,1)}) %all-gather.9.cloned.1.call-update) | async-done | bytes 4194320 | tf_op jit(solution)/shard_map/all_gather | solution.py:135
  123.1 5.7 fusion.70
  130.3 29.7 %while.33 = (s32[]{:T(128)}, bf16[4,512,4,64]{1,3,2,0:T(8,128)(2,1)}, f32[4,4,512]{2,1,0:T(4,128)S(1)}, s32[4]{0:T(128)S(1)}, bf16[2048,4,64]{0,2,1:T(8,128)(2,1...) while((s32[]{:T(128)}, ...), condition=%wide.region_5.6_spmd, body=%wide.region_2.5_spmd.sunk | while | flops 553646080 | bytes 35455444 | solution.py:63
  160.1 2.8 copy.30
  164.1 5.6 fusion.104
  171.0 8.8 all-gather.1
  179.7 133.2 %reduce-scatter.9.cloned.1.call-done = f32[512,1024]{1,0:T(8,128)} async-done(((f32[2048,1024]{1,0:T(8,128)}), f32[512,1024]{1,0:T(8,128)}) %reduce-scatter.9.cloned.1.call-update) | async-done | bytes 2097168 | tf_op jit(solution)/shard_map/reduce_scatter | solution.py:146
  312.9 2.1 fusion.103
  318.0 25.6 %collective-permute-done = bf16[512,1024]{1,0:T(8,128)(2,1)S(1)} collective-permute-done((bf16[512,1024]{1,0:T(8,128)(2,1)}, bf16[512,1024]{1,0:T(8,128)(2,1)S(1)}, u32[]{:S(2)}, u32[]{:S(2)}) %collective-permute-start) | collective-permute-done | bytes 1048608 | tf_op jit(solution)/shard_map/ppermute | solution.py:178
  344.6 25.7 %collective-permute-done.1 = bf16[512,1024]{1,0:T(8,128)(2,1)} collective-permute-done((bf16[512,1024]{1,0:T(8,128)(2,1)S(1)}, bf16[512,1024]{1,0:T(8,128)(2,1)}, u32[]{:S(2)}, u32[]{:S(2)}) %collective-permute-start.1) | collective-permute-done | bytes 1048608 | tf_op jit(solution)/shard_map/ppermute | solution.py:178
  370.6 36.0 %collective-permute-done.2 = bf16[512,1024]{1,0:T(8,128)(2,1)} collective-permute-done((bf16[512,1024]{1,0:T(8,128)(2,1)}, bf16[512,1024]{1,0:T(8,128)(2,1)}, u32[]{:S(2)}, u32[]{:S(2)}) %collective-permute-start.2) | collective-permute-done | bytes 1048608 | tf_op jit(solution)/shard_map/ppermute | solution.py:178
  406.5 2.3 constant_dynamic-update-slice_fusion.7
  408.9 2.4 constant_dynamic-update-slice_fusion.6
  411.3 2.3 constant_dynamic-update-slice_fusion.5
  414.6 2.3 constant_dynamic-update-slice_fusion.3
  416.9 2.3 constant_dynamic-update-slice_fusion.2
  421.3 8.0 fusion.74
  429.3 34.4 %all-gather.13.cloned.1.call-done = bf16[2048,1024]{1,0:T(8,128)(2,1)} async-done(((bf16[512,1024]{1,0:T(8,128)(2,1)}), bf16[2048,1024]{1,0:T(8,128)(2,1)}) %all-gather.13.cloned.1.call-update) | async-done | bytes 4194320 | tf_op jit(solution)/shard_map/all_gather | solution.py:154
  463.7 8.5 fusion.66
  472.3 12.5 %multiply_bitcast_fusion = (f32[2048,1,656]{0,2,1:T(8,128)}, f32[2048,656]{0,1:T(8,128)S(1)}) fusion(f32[2048,656]{0,1:T(8,128)S(1)} %copy-done.6, f32[2048,2,656]{0,2,1:T(8,128)S(1)} %fusion.66), kind=kLoop, calls=%fused_computation.65 | loop fusion | flops 87326720 | bytes 21495808 | tf_op jit(solution)/shard_map/transpose(jvp())/broadcast_in_dim | solution.py:34
  484.8 5.3 fusion.51
  490.1 13.6 %convolution_bitcast_fusion.1 = f32[2048,1024]{1,0:T(8,128)} fusion(bf16[1024,2,656]{0,2,1:T(8,128)(2,1)} %all-gather.15.cloned.1.call-done, f32[2048,1,656]{0,2,1:T(8,128)} %get-tuple-element.379, f32[2048,1,656]{0,2,1:T(8,128)} %get-tuple-element.371), kind=kOutput, calls=%fused_computation.82 | convolution fusion | flops 5508300800 | bytes 21823488 | tf_op jit(solution)/shard_map/tcf,dcf->td/dot_general | solution.py:190
  503.6 11.9 reduce-scatter.11.cloned.1.call-start
  515.5 7.6 convolution_convert_fusion
  523.2 123.2 %reduce-scatter.13.cloned.1.call-done = f32[512,1024]{1,0:T(8,128)} async-done(((f32[2048,1024]{1,0:T(8,128)}), f32[512,1024]{1,0:T(8,128)}) %reduce-scatter.13.cloned.1.call-update) | async-done | bytes 2097168 | tf_op jit(solution)/shard_map/reduce_scatter | solution.py:189
  646.5 2.8 multiply_reduce_fusion.2
  649.3 77.0 %reduce-scatter.11.cloned.1.call-done = bf16[512,1024]{1,0:T(8,128)(2,1)} async-done(((bf16[2048,1024]{1,0:T(8,128)(2,1)}), bf16[512,1024]{1,0:T(8,128)(2,1)}) %reduce-scatter.11.cloned.1.call-update) | async-done | bytes 1048592 | tf_op jit(solution)/shard_map/reduce_scatter | solution.py:157
  726.3 3.7 fusion.101
  732.6 81.4 %all-gather.19.cloned.1.call-done = bf16[2048,1024]{1,0:T(8,128)(2,1)} async-done(((bf16[512,1024]{1,0:T(8,128)(2,1)}), bf16[2048,1024]{1,0:T(8,128)(2,1)}) %all-gather.19.cloned.1.call-update) | async-done | bytes 4194320 | tf_op jit(solution)/shard_map/all_gather | solution.py:199
  814.0 4.6 convolution_convert_fusion.1
  822.0 53.8 %while.34 = (s32[]{:T(128)}, f32[2048,4,64]{0,2,1:T(8,128)}, f32[2048,4,64]{0,2,1:T(8,128)S(1)}, f32[2048,4,64]{0,2,1:T(8,128)}, bf16[2048,4,64]{0,2,1:T(8,128)(...) while((s32[]{:T(128)}, f32[2048,4,64]{0,2,1:T(8,128)}, ...), condition=%wide.region_15.16_spmd, body=%wide.region_13.15_spmd.sunk | while | flops 1368258560 | bytes 95478312 | solution.py:118
  822.0 2.4 fusion.146
  826.3 2.9 multiply_reduce_fusion.8
  829.2 2.0 multiply_convert_fusion.4
  833.2 2.2 fusion.147
  835.4 2.4 fusion.146
  839.8 2.8 multiply_reduce_fusion.8
  842.6 2.0 multiply_convert_fusion.4
  846.6 2.2 fusion.147
  848.9 2.4 fusion.146
  853.2 2.9 multiply_reduce_fusion.8
  860.1 2.3 fusion.147
  862.3 2.4 fusion.146
  866.7 2.8 multiply_reduce_fusion.8
  873.5 2.2 fusion.147
  878.8 3.3 multiply_add_fusion.3
  884.3 9.1 convolution_bitcast_fusion
  893.7 7.4 fusion.72
  901.2 11.3 fusion.64
  913.7 4.4 fusion.105
  918.3 7.7 fusion.68
  927.3 109.3 %reduce-scatter.15.cloned.1.call-done = f32[512,1024]{1,0:T(8,128)} async-done(((f32[2048,1024]{1,0:T(8,128)}), f32[512,1024]{1,0:T(8,128)}) %reduce-scatter.15.cloned.1.call-update) | async-done | bytes 2097168 | tf_op jit(solution)/shard_map/reduce_scatter | solution.py:217
  1036.6 2.1 fusion.85
  1038.7 2.6 fusion.83
  1041.2 13.7 %all-reduce.8 = (f32[1024]{0:T(1024)S(1)}, f32[1024]{0:T(1024)S(1)}) all-reduce(f32[1024]{0:T(1024)S(1)} %get-tuple-element.329, f32[1024]{0:T(1024)S(1)} %copy-done.34), channel_id=10, replica_groups=mesh['dp'=8,'tensor'=4] {'dp'}, use_global_device_ids=true, to_apply=%region_24.25.clone | all-reduce | flops 2048 | bytes 16384
  1055.1 12.1 all-reduce.9
  1067.2 3.2 add_convert_fusion.1
  1070.4 15.9 %reduce-scatter.23.cloned.1.call-done = f32[656,128]{1,0:T(8,128)} async-done(((f32[656,1024]{1,0:T(8,128)}), f32[656,128]{1,0:T(8,128)}) %reduce-scatter.23.cloned.1.call-update) | async-done | bytes 335888 | tf_op jit(solution)/shard_map/reduce_scatter | solution.py:230
  1086.4 61.5 %reduce-scatter.21.cloned.1.call-done = f32[128,2,656]{0,2,1:T(8,128)} async-done(((f32[1024,2,656]{0,2,1:T(8,128)}), f32[128,2,656]{0,2,1:T(8,128)}) %reduce-scatter.21.cloned.1.call-update) | async-done | bytes 671760 | tf_op jit(solution)/shard_map/reduce_scatter | solution.py:229
  1147.9 40.1 %reduce-scatter.19.cloned.1.call-done = f32[256,128]{1,0:T(8,128)} async-done(((f32[256,1024]{1,0:T(8,128)}), f32[256,128]{1,0:T(8,128)}) %reduce-scatter.19.cloned.1.call-update) | async-done | bytes 131088 | tf_op jit(solution)/shard_map/reduce_scatter | solution.py:228
  1188.0 50.5 %reduce-scatter.17.cloned.1.call-done = f32[128,3,256]{2,0,1:T(8,128)} async-done(((f32[1024,3,256]{2,0,1:T(8,128)}), f32[128,3,256]{2,0,1:T(8,128)}) %reduce-scatter.17.cloned.1.call-update) | async-done | bytes 393232 | tf_op jit(solution)/shard_map/reduce_scatter | solution.py:227
  (219 shorter events, 79.2 us)
Async XLA Ops:
  7.2 18.1 %copy-start.29 = (bf16[256,128]{1,0:T(8,128)(2,1)S(1)}, bf16[256,128]{1,0:T(8,128)(2,1)}, u32[]{:S(2)}) copy-start(bf16[256,128]{1,0:T(8,128)(2,1)} %param.14) | copy-start | bytes 196612
  7.2 32.8 %all-gather.11.cloned.1.call-start = ((), (), s32[]{:S(2)}) async-start(), calls=%async_computation.9 | async-start | bytes 1769472 | tf_op jit(solution)/shard_map/all_gather | solution.py:123
  9.0 114.1 %all-gather.9.cloned.1.call-start = ((), (), s32[]{:S(2)}) async-start(), calls=%async_computation.8 | async-start | bytes 5242880 | tf_op jit(solution)/shard_map/all_gather | solution.py:135
  19.4 5.9 copy-start.25
  20.8 4.4 copy-start.27
  22.5 2.7 copy-start.32
  22.5 2.7 copy-start.30
  25.1 287.8 %reduce-scatter.9.cloned.1.call-start = ((), (), s32[]{:S(2)}) async-start(), calls=%async_computation.10 | async-start | bytes 10485760 | tf_op jit(solution)/shard_map/reduce_scatter | solution.py:146
  38.2 91.3 %copy-start.17 = (f32[2048,32]{0,1:T(8,128)}, f32[2048,32]{0,1:T(8,128)S(1)}, u32[]{:S(2)}) copy-start(f32[2048,32]{0,1:T(8,128)S(1)} %get-tuple-element.396) | copy-start | bytes 786436
  38.2 91.3 %copy-start.19 = (f32[2048,32]{0,1:T(8,128)}, f32[2048,32]{0,1:T(8,128)S(1)}, u32[]{:S(2)}) copy-start(f32[2048,32]{0,1:T(8,128)S(1)} %get-tuple-element.397) | copy-start | bytes 786436
  133.0 1.9 copy-start.23
  140.4 1.9 copy-start.23
  147.9 1.9 copy-start.23
  155.3 1.9 copy-start.23
  160.1 9.7 copy-start.3
  160.1 9.7 copy-start.5
  169.8 251.5 %all-gather.17.cloned.1.call-start = ((), (), s32[]{:S(2)}) async-start(), calls=%async_computation.13 | async-start | bytes 1511424 | tf_op jit(solution)/shard_map/all_gather | solution.py:126
  170.3 258.9 %all-gather.15.cloned.1.call-start = ((), (), s32[]{:S(2)}) async-start(), calls=%async_computation.12 | async-start | bytes 3022848 | tf_op jit(solution)/shard_map/all_gather | solution.py:125
  170.9 292.8 %all-gather.13.cloned.1.call-start = ((), (), s32[]{:S(2)}) async-start(), calls=%async_computation.11 | async-start | bytes 5242880 | tf_op jit(solution)/shard_map/all_gather | solution.py:154
  316.7 329.7 %reduce-scatter.13.cloned.1.call-start = ((), (), s32[]{:S(2)}) async-start(), calls=%async_computation.15 | async-start | bytes 10485760 | tf_op jit(solution)/shard_map/reduce_scatter | solution.py:189
  316.8 26.8 %collective-permute-start = (bf16[512,1024]{1,0:T(8,128)(2,1)}, bf16[512,1024]{1,0:T(8,128)(2,1)S(1)}, u32[]{:S(2)}, u32[]{:S(2)}) collective-permute-start(bf16[512,1024]{1,0:T(8,128)(2,1)} %param.19), channel_id=1, source_target_pairs={{0,1},{1,2},{2,3},{3,0},{4,5},{5,6},{6,7},{7,4},{8,9},{9,10},{10,1... | collective-permute-start | bytes 3145736 | tf_op jit(solution)/shard_map/ppermute | solution.py:178
  344.6 25.7 %collective-permute-start.1 = (bf16[512,1024]{1,0:T(8,128)(2,1)S(1)}, bf16[512,1024]{1,0:T(8,128)(2,1)}, u32[]{:S(2)}, u32[]{:S(2)}) collective-permute-start(bf16[512,1024]{1,0:T(8,128)(2,1)S(1)} %collective-permute-done), channel_id=1, source_target_pairs={{0,1},{1,2},{2,3},{3,0},{4,5},{5,6},{6,7},{7,4},{8,9},{9,10},{10,1... | collective-permute-start | bytes 3145736 | tf_op jit(solution)/shard_map/ppermute | solution.py:178
  370.3 36.2 %collective-permute-start.2 = (bf16[512,1024]{1,0:T(8,128)(2,1)}, bf16[512,1024]{1,0:T(8,128)(2,1)}, u32[]{:S(2)}, u32[]{:S(2)}) collective-permute-start(bf16[512,1024]{1,0:T(8,128)(2,1)} %collective-permute-done.1), channel_id=1, source_target_pairs={{0,1},{1,2},{2,3},{3,0},{4,5},{5,6},{6,7},{7,4},{8,9},{9,10},{10,1... | collective-permute-start | bytes 3145736 | tf_op jit(solution)/shard_map/ppermute | solution.py:178
  370.6 43.0 %copy-start.9 = (bf16[512,1024]{1,0:T(8,128)(2,1)S(1)}, bf16[512,1024]{1,0:T(8,128)(2,1)}, u32[]{:S(2)}) copy-start(bf16[512,1024]{1,0:T(8,128)(2,1)} %param.19) | copy-start | bytes 3145732
  408.9 10.3 copy-start.16
  463.7 8.6 copy-start.6
  503.6 222.6 %reduce-scatter.11.cloned.1.call-start = ((), (), s32[]{:S(2)}) async-start(), calls=%async_computation.14 | async-start | bytes 5242880 | tf_op jit(solution)/shard_map/reduce_scatter | solution.py:157
  523.2 290.9 %all-gather.19.cloned.1.call-start = ((), (), s32[]{:S(2)}) async-start(), calls=%async_computation.16 | async-start | bytes 5242880 | tf_op jit(solution)/shard_map/all_gather | solution.py:199
  726.3 5.0 copy-start.10
  730.0 1.3 copy-start.7
  732.6 304.0 %reduce-scatter.15.cloned.1.call-start = ((), (), s32[]{:S(2)}) async-start(), calls=%async_computation.17 | async-start | bytes 10485760 | tf_op jit(solution)/shard_map/reduce_scatter | solution.py:217
  822.0 2.4 copy-start.1
  822.0 2.4 copy-start.11
  824.4 1.9 copy-start.4
  826.3 2.9 copy-start.2
  835.4 2.4 copy-start.1
  835.4 2.4 copy-start.11
  837.8 1.9 copy-start.4
  839.8 2.9 copy-start.2
  848.9 2.4 copy-start.1
  848.9 2.4 copy-start.11
  851.3 1.9 copy-start.4
  853.2 2.9 copy-start.2
  862.3 2.4 copy-start.1
  862.3 2.4 copy-start.11
  864.7 1.9 copy-start.4
  866.7 2.9 copy-start.2
  875.7 3.1 copy-start.18
  882.1 1.5 copy-start.14
  884.2 9.1 copy-start.22
  893.4 193.0 %reduce-scatter.23.cloned.1.call-start = ((), (), s32[]{:S(2)}) async-start(), calls=%async_computation.21 | async-start | bytes 3022848 | tf_op jit(solution)/shard_map/reduce_scatter | solution.py:230
  901.1 246.7 %reduce-scatter.21.cloned.1.call-start = ((), (), s32[]{:S(2)}) async-start(), calls=%async_computation.20 | async-start | bytes 6045696 | tf_op jit(solution)/shard_map/reduce_scatter | solution.py:229
  912.5 5.8 copy-start.20
  912.5 5.8 copy-start.21
  912.5 275.5 %reduce-scatter.19.cloned.1.call-start = ((), (), s32[]{:S(2)}) async-start(), calls=%async_computation.19 | async-start | bytes 1179648 | tf_op jit(solution)/shard_map/reduce_scatter | solution.py:228
  918.1 7.9 copy-start.36
  918.2 118.4 %copy-start = (bf16[512,1024]{1,0:T(8,128)(2,1)S(1)}, bf16[512,1024]{1,0:T(8,128)(2,1)}, u32[]{:S(2)}) copy-start(bf16[512,1024]{1,0:T(8,128)(2,1)} %param.12) | copy-start | bytes 3145732
  918.2 118.4 %copy-start.26 = (f32[8,1,128]{2,1,0:T(1,128)S(1)}, f32[8,1,128]{2,1,0:T(1,128)}, u32[]{:S(2)}) copy-start(f32[8,1,128]{2,1,0:T(1,128)} %copy-done.25) | copy-start | bytes 12292
  918.2 118.4 %copy-start.28 = (f32[512]{0:T(512)S(1)}, f32[512]{0:T(512)}, u32[]{:S(2)}) copy-start(f32[512]{0:T(512)} %copy-done.27) | copy-start | bytes 6148
  918.2 320.2 %reduce-scatter.17.cloned.1.call-start = ((), (), s32[]{:S(2)}) async-start(), calls=%async_computation.18 | async-start | bytes 3538944 | tf_op jit(solution)/shard_map/reduce_scatter | solution.py:227
  926.0 112.7 %copy-start.33 = (f32[512]{0:T(512)S(1)}, f32[512]{0:T(512)}, u32[]{:S(2)}) copy-start(f32[512]{0:T(512)} %copy-done.32) | copy-start | bytes 6148
  926.0 112.7 %copy-start.31 = (f32[512]{0:T(512)S(1)}, f32[512]{0:T(512)}, u32[]{:S(2)}) copy-start(f32[512]{0:T(512)} %copy-done.30) | copy-start | bytes 6148
  926.0 115.3 %copy-start.34 = (f32[1024]{0:T(1024)S(1)}, f32[1024]{0:T(1024)}, u32[]{:S(2)}) copy-start(f32[1024]{0:T(1024)} %get-tuple-element.327) | copy-start | bytes 12292
  926.0 141.2 %copy-start.8 = (f32[512,1024]{1,0:T(8,128)S(1)}, f32[512,1024]{1,0:T(8,128)}, u32[]{:S(2)}) copy-start(f32[512,1024]{1,0:T(8,128)} %copy-done.7) | copy-start | bytes 6291460
  (8 other events, 8.3 us)
Sparse Core Ops, SparseCore 0:
  10.5 29.4 all-gather.10
  42.1 80.9 all-gather.8
  169.9 142.9 reduce-scatter.8
  314.6 25.5 all-gather.16
  342.0 30.7 all-gather.14
  374.8 88.8 all-gather.12
  503.8 142.6 reduce-scatter.12
  648.7 77.4 reduce-scatter.10
  732.7 81.2 all-gather.18
  893.5 142.9 reduce-scatter.14
  1041.0 45.3 reduce-scatter.22
  1090.6 57.2 reduce-scatter.20
  1151.9 35.9 reduce-scatter.18
  1192.2 46.2 reduce-scatter.16
